TPU v7x, 512 devices: a whole 4x8x8 slice. The times are simulated.
512 devices in a mesh: sec: 32 (over x, y), term: 16 (over z, core).
Axes of the slice: x: 4, y: 8, z: 8, core: 2. Of those that a mesh axis runs over, the one named last changes fastest.
Arguments:
- vectors: bfloat16 [2, 32, 4, 256, 256], P(None, 'sec'), may hold values from -6 to 6
- left_ops: bfloat16 [48, 32, 256, 256], P('term', 'sec'), may hold values from -0.375 to 0.375
- right_ops: bfloat16 [48, 32, 256, 256], P('term', 'sec'), may hold values from -0.0546875 to 0.0546875
- offsets: int32 [48, 4], P('term'), may hold values from 0 to 31, as said below
Outputs:
- products: bfloat16 [2, 32, 4, 256, 256], P(None, 'sec', None, 'term')
- rayleigh: float32 [2, 2], replicated
Inputs may be any that keep to these rules, and one draw needn't show every extreme that they name: Each term's 4 offsets are distinct, and every shift from 0 to 31 occurs for some term and pair.
All inputs are finite; a program needn't handle non-finite values.
Results may differ from a plain program's by a relative error of at most 0.015.
Values may be sent and summed in bfloat16 or wider, within the bound.
A program may use at most 64 MiB of HBM per device.

v0:
```python
import jax
import jax.numpy as jnp
from jax import lax
from jax.sharding import PartitionSpec as P


def pick_blocks(carried, piece, needed):
    piece_width = piece.shape[1]
    chosen_list = []
    for pair_index in range(needed.shape[1]):
        offset_in = needed[:, pair_index]
        inside = (offset_in >= 0) & (offset_in < piece_width)
        clipped = jnp.clip(offset_in, 0, piece_width - 1)
        candidate = jnp.take_along_axis(piece, clipped[:, None, None, None], axis=1)[:, 0]
        chosen_list.append(jnp.where(inside[:, None, None], candidate, carried[pair_index]))
    return jnp.stack(chosen_list)


def local(vectors, left_ops, right_ops, offsets):
    sectors = lax.axis_size("sec")
    my_sector = lax.axis_index("sec")
    needed = (my_sector + offsets) % sectors
    local_vectors = vectors[:, 0]
    inner_part = jnp.einsum(
        "tab,ipbc->tipac", left_ops[:, 0], local_vectors, preferred_element_type=jnp.float32
    ).astype(jnp.bfloat16)
    pair_count = offsets.shape[1]
    own_right = right_ops[:, 0]
    empty_blocks = jnp.zeros((pair_count,) + own_right.shape, jnp.bfloat16)
    picked = pick_blocks(empty_blocks, lax.all_gather(right_ops, "sec", axis=1, tiled=True), needed)
    partial_value = jnp.einsum(
        "tipac,ptcd->ipad", inner_part, picked, preferred_element_type=jnp.float32
    )
    rows_share = local_vectors.shape[2] // lax.axis_size("term")
    row_start = lax.axis_index("term") * rows_share
    vector_share = lax.dynamic_slice_in_dim(local_vectors, row_start, rows_share, 2).astype(
        jnp.float32
    )
    square_part = jnp.sum(vector_share * vector_share, axis=(1, 2, 3))
    shares = lax.psum_scatter(partial_value, "term", scatter_dimension=2, tiled=True)
    gram_part = jnp.einsum("ipab,jpab->ij", vector_share, shares)
    gram_matrix, squares = lax.psum((gram_part, square_part), ("sec", "term"))
    rayleigh = gram_matrix / jnp.sqrt(squares[:, None] * squares[None, :])
    return (shares.astype(jnp.bfloat16)[:, None], rayleigh)


def solution(mesh):
    in_specs = (
        P(None, "sec", None, None, None),
        P("term", "sec", None, None),
        P("term", "sec", None, None),
        P("term", None),
    )
    out_specs = (P(None, "sec", None, "term", None), P())
    return jax.shard_map(local, mesh=mesh, in_specs=in_specs, out_specs=out_specs, check_vma=False)
```

profile of v0, /device:TPU:1, one launch (start us, length us, event | category | flops | bytes accessed | tf_op | source)
XLA Modules:
  0.0 334.2 jit_solution(14229687823892872018)
XLA Ops:
  7.2 0.7 all-gather.2.cloned.1.call-update
  7.9 1.3 dynamic-slice.1
  9.8 0.7 add_select_fusion
  10.5 0.2 clamp_reduce_fusion.3
  10.8 0.2 and_reduce_fusion.3
  11.1 0.3 multiply_reduce_fusion
  11.4 129.7 %all-gather.2.cloned.1.call-done = bf16[3,32,256,256]{3,2,1,0:T(8,128)(2,1)} async-done(((bf16[3,1,256,256]{3,2,1,0:T(8,128)(2,1)}), bf16[3,32,256,256]{3,2,1,0:T(8,128)(2,1)}) %all-gather.2.cloned.1.call-update) | async-done | bytes 12582928 | tf_op jit(solution)/shard_map/all_gather | solution.py:30
  141.1 5.2 %gather_fusion.3 = bf16[3,256,256]{2,1,0:T(8,128)(2,1)S(1)} fusion(bf16[3,32,256,256]{3,2,1,0:T(8,128)(2,1)} %all-gather.2.cloned.1.call-done, s32[3]{0:T(128)S(1)} %or_bitcast_fusion), kind=kCustom, calls=%fused_computation.3.clone | custom fusion | bytes 786456 | tf_op jit(solution)/shard_map/jit(take_along_axis)/gather | solution.py:14
  146.2 0.2 copy.19
  146.4 5.2 %gather_fusion.2 = bf16[3,256,256]{2,1,0:T(8,128)(2,1)S(1)} fusion(bf16[3,32,256,256]{3,2,1,0:T(8,128)(2,1)} %all-gather.2.cloned.1.call-done, s32[3]{0:T(128)S(1)} %or_bitcast_fusion.1), kind=kCustom, calls=%fused_computation.2.clone | custom fusion | bytes 786456 | tf_op jit(solution)/shard_map/jit(take_along_axis)/gather | solution.py:14
  151.6 0.2 copy.18
  151.7 5.2 %gather_fusion.1 = bf16[3,256,256]{2,1,0:T(8,128)(2,1)S(1)} fusion(bf16[3,32,256,256]{3,2,1,0:T(8,128)(2,1)} %all-gather.2.cloned.1.call-done, s32[3]{0:T(128)S(1)} %or_bitcast_fusion.2), kind=kCustom, calls=%fused_computation.1.clone | custom fusion | bytes 786456 | tf_op jit(solution)/shard_map/jit(take_along_axis)/gather | solution.py:14
  157.0 0.2 copy.17
  157.1 5.2 %gather_fusion = bf16[3,256,256]{2,1,0:T(8,128)(2,1)S(1)} fusion(bf16[3,32,256,256]{3,2,1,0:T(8,128)(2,1)} %all-gather.2.cloned.1.call-done, s32[3]{0:T(128)S(1)} %or_bitcast_fusion.3), kind=kCustom, calls=%fused_computation.clone | custom fusion | bytes 786456 | tf_op jit(solution)/shard_map/jit(take_along_axis)/gather | solution.py:14
  162.3 0.2 copy.16
  162.9 3.2 fusion.5
  166.2 2.2 copy.22
  168.4 59.1 %all-reduce.3 = bf16[2,4,256,256]{3,1,0,2:T(4,128)(2,1)} all-reduce(f32[2,4,256,256]{3,1,0,2:T(4,128)S(1)} %copy.22), channel_id=2, replica_groups=mesh['sec'=32,'term'=16] {'term'}, use_global_device_ids=true, to_apply=%region_0.2.clone | all-reduce | flops 524288 | bytes 3145728
  227.6 0.9 fusion.29
  228.5 0.9 constant_dynamic-slice_fusion
  229.3 0.3 convolution_bitcast_fusion
  229.6 0.7 copy.25
  230.3 96.4 %all-reduce.1 = (f32[2,2]{1,0:T(2,128)S(1)}, f32[2]{0:T(128)S(1)}) all-reduce(f32[2,2]{1,0:T(2,128)S(1)} %convolution_bitcast_fusion, f32[2]{0:T(128)S(1)} %multiply_reduce_fusion), channel_id=1, replica_groups=mesh['sec'=32,'term'=16] {'sec','term'}, use_global_device_ids=true, to_apply=%region_1.3 | all-reduce | flops 6 | bytes 48 | tf_op jit(solution)/shard_map/psum | solution.py:42
  326.7 0.6 rsqrt_multiply_fusion
  (20 shorter events, 0.6 us)
Async XLA Ops:
  7.2 3.9 %copy-start = (bf16[2,1,4,256,256]{4,3,2,1,0:T(8,128)(2,1)S(1)}, bf16[2,1,4,256,256]{4,3,2,1,0:T(8,128)(2,1)}, u32[]{:S(2)}) copy-start(bf16[2,1,4,256,256]{4,3,2,1,0:T(8,128)(2,1)} %param.6) | copy-start | bytes 3145732
  7.2 133.9 %all-gather.2.cloned.1.call-start = ((), (), s32[]{:S(2)}) async-start(), calls=%async_computation | async-start | bytes 12976128 | tf_op jit(solution)/shard_map/all_gather | solution.py:30
  151.7 11.2 %copy-start.1 = (bf16[3,1,256,256]{3,2,1,0:T(8,128)(2,1)S(1)}, bf16[3,1,256,256]{3,2,1,0:T(8,128)(2,1)}, u32[]{:S(2)}) copy-start(bf16[3,1,256,256]{3,2,1,0:T(8,128)(2,1)} %param.7) | copy-start | bytes 1179652
Sparse Core Ops, SparseCore 0:
  11.2 129.8 all-gather.1
where the time goes:
time: 335 us; the launch traced here: 334 us
  blocking collectives  156 us (47%)
  waiting for transfers between devices  130 us (39%)
  local copies, waits for them, and re-layouts  27.3 us (8%)
  between operations  14.9 us (4%)
  matrix products  3.56 us (1%)
    all_gather x1, waiting for transfers between devices, local(): lax.all_gather(right_ops, 'sec', axis=1, tiled=True)  130 us
    psum x1, blocking collectives, local(): gram_matrix, squares = lax.psum((gram_part, square_part), ('sec', 'term'))  96.4 us
    unnamed x1, blocking collectives  59.1 us
    gather x8, local copies, waits for them, and re-layouts, pick_blocks(): jnp.take_along_axis(piece, clipped[:, None, None, None], axis=1)[:, 0]  21.3 us
  transfers between devices with their start and end apart: 1, of which 1 were waited for; matrix products, arithmetic and copies ran while one was open for 1% of the time, Pallas kernels for 0%

commit v1 on v0

--- a/solution.py
+++ b/solution.py
@@ -27,7 +27,13 @@
     pair_count = offsets.shape[1]
     own_right = right_ops[:, 0]
     empty_blocks = jnp.zeros((pair_count,) + own_right.shape, jnp.bfloat16)
-    picked = pick_blocks(empty_blocks, lax.all_gather(right_ops, "sec", axis=1, tiled=True), needed)
+    picked = pick_blocks(
+        empty_blocks,
+        jnp.concatenate(
+            lax.all_to_all(jnp.stack([right_ops] * lax.axis_size("sec")), "sec", 0, 0), axis=1
+        ),
+        needed,
+    )
     partial_value = jnp.einsum(
         "tipac,ptcd->ipad", inner_part, picked, preferred_element_type=jnp.float32
     )

time: 335 us -> 528 us (1.58)
  waiting for transfers between devices: 130 us -> 282 us
  blocking collectives: 156 us -> 182 us
  local copies, waits for them, and re-layouts: 27.3 us -> 44.9 us
  between operations: 14.9 us -> 1.49 us
  starting transfers between devices: 0.04 us -> 10.7 us
    all_to_all x0 -> x1, waiting for transfers between devices: none -> 282 us  [local(): lax.all_to_all(jnp.stack([right_ops] * lax.axis_size('sec')), 'sec', 0, 0)]
    all_gather x1 -> x0, waiting for transfers between devices: 130 us -> none  [local(): lax.all_gather(right_ops, 'sec', axis=1, tiled=True)]
    psum x1, blocking collectives: 96.4 us -> 121 us  [local(): gram_matrix, squares = lax.psum((gram_part, square_part), ('sec', 'term'))]
    all_to_all x0 -> x1, starting transfers between devices: none -> 10.7 us  [local(): lax.all_to_all(jnp.stack([right_ops] * lax.axis_size('sec')), 'sec', 0, 0)]
    all_to_all x0 -> x1, local copies, waits for them, and re-layouts: none -> 10.5 us  [local(): lax.all_to_all(jnp.stack([right_ops] * lax.axis_size('sec')), 'sec', 0, 0)]
    another operation x0 -> x1, local copies, waits for them, and re-layouts: none -> 7.11 us  [local(): jnp.stack([right_ops] * lax.axis_size('sec'))]
  transfers between devices with their start and end apart: 1 -> 1, of which waited for: 1 -> 1; matrix products, arithmetic and copies ran while one was open for 1% -> 0% of each run, Pallas kernels for 0% -> 0%
where the time goes in v1:
time: 528 us
  waiting for transfers between devices  282 us (53%)
  blocking collectives  182 us (34%)
  local copies, waits for them, and re-layouts  44.9 us (9%)
  starting transfers between devices  10.7 us (2%)
    all_to_all x1, waiting for transfers between devices, local(): lax.all_to_all(jnp.stack([right_ops] * lax.axis_size('sec')), 'sec', 0, 0)  282 us
    psum x1, blocking collectives, local(): gram_matrix, squares = lax.psum((gram_part, square_part), ('sec', 'term'))  121 us
    unnamed x1, blocking collectives  60.6 us
    gather x8, local copies, waits for them, and re-layouts, pick_blocks(): jnp.take_along_axis(piece, clipped[:, None, None, None], axis=1)[:, 0]  21.3 us
    all_to_all x1, starting transfers between devices, local(): lax.all_to_all(jnp.stack([right_ops] * lax.axis_size('sec')), 'sec', 0, 0)  10.7 us
  transfers between devices with their start and end apart: 1, of which 1 were waited for; matrix products, arithmetic and copies ran while one was open for 0% of the time, Pallas kernels for 0%

profile of v1, /device:TPU:1, one launch (start us, length us, event | category | flops | bytes accessed | tf_op | source)
XLA Modules:
  0.0 527.6 jit_solution(3318012835913415932)
XLA Ops:
  0.6 7.1 %stack.4 = bf16[32,3,1,256,256]{4,3,1,2,0:T(8,128)(2,1)} broadcast(bf16[3,256,256]{2,1,0:T(8,128)(2,1)} %bitcast.132), dimensions={1,3,4} | broadcast | bytes 12976128 | tf_op jit(solution)/shard_map/stack | solution.py:33
  7.8 10.7 %all-to-all-start = ((bf16[32,3,1,256,256]{4,3,1,2,0:T(8,128)(2,1)}), bf16[32,3,1,256,256]{4,3,1,2,0:T(8,128)(2,1)}, u32[]{:S(2)}, u32[]{:S(2)}) async-start(bf16[32,3,1,256,256]{4,3,1,2,0:T(8,128)(2,1)} %stack.4), calls=%async_computation | async-start | bytes 25165824 | tf_op jit(solution)/shard_map/all_to_all | solution.py:33
  18.5 1.3 dynamic-slice.1
  20.5 0.2 clamp_reduce_fusion.3
  20.7 0.2 and_reduce_fusion.3
  21.0 0.3 multiply_reduce_fusion
  21.3 282.2 %all-to-all-done = bf16[32,3,1,256,256]{4,3,1,2,0:T(8,128)(2,1)} async-done(((bf16[32,3,1,256,256]{4,3,1,2,0:T(8,128)(2,1)}), bf16[32,3,1,256,256]{4,3,1,2,0:T(8,128)(2,1)}, u32[]{:S(2)}, u32[]{:S(2)}) %all-to-all-start) | async-done | bytes 12582944 | tf_op jit(solution)/shard_map/all_to_all | solution.py:33
  303.6 10.5 %copy.44 = bf16[32,3,1,256,256]{4,3,0,1,2:T(8,128)(2,1)} copy(bf16[32,3,1,256,256]{4,3,1,2,0:T(8,128)(2,1)} %all-to-all-done) | data formatting | bytes 25165824 | tf_op jit(solution)/shard_map/all_to_all | solution.py:33
  314.1 5.2 gather_fusion.3
  319.3 0.2 copy.20
  319.4 5.2 gather_fusion.2
  324.6 0.2 copy.19
  324.8 5.2 gather_fusion.1
  329.9 0.2 copy.18
  330.1 5.2 gather_fusion
  335.9 4.2 fusion.5
  340.1 2.2 copy.23
  342.4 60.6 %all-reduce.3 = bf16[2,4,256,256]{3,1,0,2:T(4,128)(2,1)} all-reduce(f32[2,4,256,256]{3,1,0,2:T(4,128)S(1)} %copy.23), channel_id=2, replica_groups=mesh['sec'=32,'term'=16] {'term'}, use_global_device_ids=true, to_apply=%region_0.2.clone | all-reduce | flops 524288 | bytes 3145728
  403.0 0.9 fusion.29
  403.8 0.9 constant_dynamic-slice_fusion
  404.7 0.3 convolution_bitcast_fusion
  405.0 0.7 copy.26
  405.7 121.3 %all-reduce.1 = (f32[2,2]{1,0:T(2,128)S(1)}, f32[2]{0:T(128)S(1)}) all-reduce(f32[2,2]{1,0:T(2,128)S(1)} %convolution_bitcast_fusion, f32[2]{0:T(128)S(1)} %multiply_reduce_fusion), channel_id=1, replica_groups=mesh['sec'=32,'term'=16] {'sec','term'}, use_global_device_ids=true, to_apply=%region_1.3 | all-reduce | flops 6 | bytes 48 | tf_op jit(solution)/shard_map/psum | solution.py:48
  526.9 0.6 rsqrt_multiply_fusion
  (21 shorter events, 0.7 us)
Async XLA Ops:
  0.6 20.3 %copy-start = (bf16[2,1,4,256,256]{4,3,2,1,0:T(8,128)(2,1)S(1)}, bf16[2,1,4,256,256]{4,3,2,1,0:T(8,128)(2,1)}, u32[]{:S(2)}) copy-start(bf16[2,1,4,256,256]{4,3,2,1,0:T(8,128)(2,1)} %param.6) | copy-start | bytes 3145732
  7.8 12.7 %copy-start.1 = (s32[3,4]{1,0:T(4,128)S(1)}, s32[3,4]{1,0:T(4,128)}, u32[]{:S(2)}) copy-start(s32[3,4]{1,0:T(4,128)} %param.9) | copy-start | bytes 148
  7.8 295.8 %all-to-all-start = ((bf16[32,3,1,256,256]{4,3,1,2,0:T(8,128)(2,1)}), bf16[32,3,1,256,256]{4,3,1,2,0:T(8,128)(2,1)}, u32[]{:S(2)}, u32[]{:S(2)}) async-start(bf16[32,3,1,256,256]{4,3,1,2,0:T(8,128)(2,1)} %stack.4), calls=%async_computation | async-start | bytes 25165824 | tf_op jit(solution)/shard_map/all_to_all | solution.py:33
